TPU v7x, 256 devices: a whole 4x4x8 slice. The times are simulated.
256 devices in a mesh: pipe: 8 (over x, y_hi), ctx: 32 (over y_lo, z, core).
Axes of the slice: x: 4, y: 4 (y_hi: 2, y_lo: 2; y = y_hi * 2 + y_lo), z: 8, core: 2. Of those that a mesh axis runs over, the one named last changes fastest.
Arguments:
- stored_acts: bfloat16 [8, 4096, 1024], P('pipe', 'ctx'), may hold values from -6 to 6
- queries: bfloat16 [8, 4096, 1024], P('pipe', 'ctx'), may hold values from -40 to 40
- patch_times: int32 [8, 4096], P('pipe', 'ctx'), may hold values from 0 to 31, as said below
- key_gain: float32 [8, 1024], P('pipe'), may hold values from 0.5 to 2
- value_gain: float32 [8, 1024], P('pipe'), may hold values from 0.5 to 2
- conv_weight: bfloat16 [8, 27, 128, 128], P('pipe'), may hold values from -0.109375 to 0.109375
- prior_grad: bfloat16 [8, 4096, 1024], P('pipe', 'ctx'), may hold values from -6 to 6
- loss_grad: bfloat16 [4096, 1024], P('ctx'), may hold values from -6 to 6
Outputs:
- input_grad: bfloat16 [8, 4096, 1024], P('pipe', 'ctx')
Inputs may be any that keep to these rules, and one draw needn't show every extreme that they name: `patch_times`: within each aligned group of four patches of a sequence, no patch has a later time step than the first of the group.
All inputs are finite; a program needn't handle non-finite values.
Results may differ from a plain program's by a relative error of at most 0.012.
Values may be sent and summed in bfloat16 or wider, within the bound.
No kernel may reach another device: no remote copies, remote signals or barrier semaphores. Data moves between devices by JAX's collectives and lax.ppermute only.
A program may use at most 128 MiB of HBM per device.

v0:
```python
import math
import jax
import jax.numpy as jnp
from jax import lax
from jax.sharding import PartitionSpec as P

HEADS = 16
HEAD_DIM = 64
CHANNELS = 128
GY = 8
GZ = 8
D = 1024
FIELDS = 8


def shifted(value, axis, steps):
    count = lax.axis_size(axis)
    leading, last = (max(0, -steps), min(count, count - steps))
    return lax.ppermute(value, axis, [(source, source + steps) for source in range(leading, last)])


def padded_2(block, sides, width):
    for axis, dim in sides:
        count = lax.axis_size(axis)
        forward = [(i, i + 1) for i in range(count - 1)]
        backward = [(target, source) for source, target in forward]
        low = lax.ppermute(
            lax.slice_in_dim(block, block.shape[dim] - width, None, axis=dim), axis, forward
        )
        high = lax.ppermute(lax.slice_in_dim(block, 0, width, axis=dim), axis, backward)
        block = jnp.concatenate([low, block, high], axis=dim)
    return block


def conv_backward(extended, weight, row_count):
    planes = row_count // (GY * GZ)
    grid_field = extended.reshape(planes + 2, GY, GZ, FIELDS, CHANNELS)
    padded = jnp.pad(grid_field, ((0, 0), (1, 1), (1, 1), (0, 0), (0, 0)))
    windows = []
    for shift_x in (-1, 0, 1):
        for shift_y in (-1, 0, 1):
            for shift_z in (-1, 0, 1):
                windows.append(
                    padded[
                        1 - shift_x : 1 - shift_x + planes,
                        1 - shift_y : 1 - shift_y + GY,
                        1 - shift_z : 1 - shift_z + GZ,
                    ]
                )
    stacked = jnp.stack(windows, axis=4).reshape(row_count * FIELDS, 27 * CHANNELS)
    matrix = jnp.transpose(weight, (0, 2, 1)).reshape(27 * CHANNELS, CHANNELS)
    return jnp.dot(stacked, matrix, preferred_element_type=jnp.float32).reshape(row_count, D)


def split_heads(matrix):
    return matrix.reshape(matrix.shape[0], HEADS, matrix.shape[1] // HEADS)


def keys_values(rows_x, key_scale, value_scale):
    widened = rows_x.astype(jnp.float32)
    keyed = split_heads((widened * key_scale).astype(jnp.bfloat16))
    valued = jnp.roll(split_heads((widened * value_scale).astype(jnp.bfloat16)), HEADS // 2, axis=1)
    return (keyed, valued)


def masked_scores(query_heads, key_heads, query_times, key_times):
    scores = jnp.einsum(
        "qhe,khe->qhk", query_heads, key_heads, preferred_element_type=jnp.float32
    ) * HEAD_DIM ** (-0.5)
    visible = key_times[None, None, :] <= query_times[:, None, None]
    return jnp.where(visible, scores, -jnp.inf)


def running_stats(running, query_heads, grad_heads, query_times, key_heads, value_heads, key_times):
    running_max, running_sum, weighted = running
    scores = masked_scores(query_heads, key_heads, query_times, key_times)
    prob_grad = jnp.einsum(
        "qhe,khe->qhk", grad_heads, value_heads, preferred_element_type=jnp.float32
    )
    new_max = jnp.maximum(running_max, jnp.max(scores, axis=2))
    exponent = jnp.exp(scores - new_max[:, :, None])
    factor = jnp.exp(running_max - new_max)
    return (
        new_max,
        running_sum * factor + jnp.sum(exponent, axis=2),
        weighted * factor + jnp.sum(exponent * prob_grad, axis=2),
    )


def key_terms(
    query_heads,
    grad_heads,
    query_times,
    log_total,
    delta_rows,
    key_heads,
    value_heads,
    key_times,
    key_scale,
    value_scale,
):
    scores = masked_scores(query_heads, key_heads, query_times, key_times)
    probability = jnp.exp(scores - log_total[:, :, None])
    prob_grad = jnp.einsum(
        "qhe,khe->qhk", grad_heads, value_heads, preferred_element_type=jnp.float32
    )
    score_grad = (probability * (prob_grad - delta_rows[:, :, None])).astype(jnp.bfloat16)
    value_grad = jnp.einsum(
        "qhk,qhe->khe",
        probability.astype(jnp.bfloat16),
        grad_heads,
        preferred_element_type=jnp.float32,
    )
    key_grad = jnp.einsum(
        "qhk,qhe->khe", score_grad, query_heads, preferred_element_type=jnp.float32
    ) * HEAD_DIM ** (-0.5)
    key_count = key_heads.shape[0]
    return (
        key_grad.reshape(key_count, -1) * key_scale
        + jnp.roll(value_grad, HEADS // 2, axis=1).reshape(key_count, -1) * value_scale
    )


def on_device(
    stored_acts, queries, patch_times, key_gain, value_gain, conv_weight, prior_grad, loss_grad
):
    own_acts = stored_acts[0]
    own_queries = queries[0]
    own_times = patch_times[0].astype(jnp.float32)
    time_wire = patch_times[0].astype(jnp.bfloat16)
    key_scale = key_gain[0]
    value_scale = value_gain[0]
    row_count = own_acts.shape[0]
    feature_count = own_acts.shape[1]
    arrived = shifted(prior_grad[0], "pipe", -1)
    is_last = lax.axis_index("pipe") == lax.axis_size("pipe") - 1
    incoming = jnp.where(is_last, loss_grad, arrived)
    extended = padded_2(incoming, (("ctx", 0),), GY * GZ)
    conv_part = conv_backward(extended, conv_weight[0], row_count)
    query_heads = split_heads(own_queries)
    grad_heads = split_heads(incoming)
    start_stats = (
        jnp.full((row_count, HEADS), -1e30, jnp.float32),
        jnp.zeros((row_count, HEADS), jnp.float32),
        jnp.zeros((row_count, HEADS), jnp.float32),
    )

    def sweep_keys(running, segment):
        key_heads, value_heads = keys_values(segment[0], key_scale, value_scale)
        return (
            running_stats(
                running,
                query_heads,
                grad_heads,
                own_times,
                key_heads,
                value_heads,
                segment[1].astype(jnp.float32),
            ),
            None,
        )

    shard_part = (
        lax.all_gather(own_acts, "ctx", axis=0, tiled=True),
        lax.all_gather(time_wire, "ctx", axis=0, tiled=True),
    )
    running = start_stats
    segment_x = shard_part[0]
    length = segment_x.shape[0]
    block_size = math.gcd(length, 512)
    running, _ = lax.scan(
        sweep_keys,
        running,
        (
            segment_x.reshape(length // block_size, block_size, feature_count),
            shard_part[1].reshape(length // block_size, block_size),
        ),
    )
    running_max, running_sum, weighted = running
    log_total = running_max + jnp.log(running_sum)
    delta_rows = weighted / running_sum
    all_total, all_delta, all_times = (
        lax.all_gather(log_total, "ctx", axis=0, tiled=True),
        lax.all_gather(delta_rows, "ctx", axis=0, tiled=True),
        lax.all_gather(own_times, "ctx", axis=0, tiled=True),
    )
    own_keys, own_values = keys_values(own_acts, key_scale, value_scale)

    def sweep_queries(accumulated, segment):
        segment_q, segment_g, segment_times, segment_total, segment_delta = segment
        return (
            accumulated
            + key_terms(
                split_heads(segment_q),
                split_heads(segment_g),
                segment_times,
                segment_total,
                segment_delta,
                own_keys,
                own_values,
                own_times,
                key_scale,
                value_scale,
            ),
            None,
        )

    accumulated = jnp.zeros((row_count, feature_count), jnp.float32)
    shard_part = (
        lax.all_gather(own_queries, "ctx", axis=0, tiled=True),
        lax.all_gather(incoming, "ctx", axis=0, tiled=True),
    )
    length = shard_part[0].shape[0]
    block_size = math.gcd(length, 512)
    block_count = length // block_size
    segments = (
        shard_part[0].reshape(block_count, block_size, feature_count),
        shard_part[1].reshape(block_count, block_size, feature_count),
        all_times.reshape(block_count, block_size),
        all_total.reshape(block_count, block_size, HEADS),
        all_delta.reshape(block_count, block_size, HEADS),
    )
    accumulated, _ = lax.scan(sweep_queries, accumulated, segments)
    return (conv_part + accumulated).astype(jnp.bfloat16)[None]


def solution(mesh):
    in_specs = (
        P("pipe", "ctx", None),
        P("pipe", "ctx", None),
        P("pipe", "ctx"),
        P("pipe", None),
        P("pipe", None),
        P("pipe", None, None, None),
        P("pipe", "ctx", None),
        P("ctx", None),
    )
    out_specs = P("pipe", "ctx", None)
    return jax.shard_map(
        on_device, mesh=mesh, in_specs=in_specs, out_specs=out_specs, check_vma=False
    )
```

profile of v0, /device:TPU:29, one launch (start us, length us, event | category | flops | bytes accessed | tf_op | source)
XLA Modules:
  0.0 412.9 jit_solution(16347624726571813158)
XLA Ops:
  8.4 2.9 collective-permute-start
  12.4 7.5 %collective-permute-done = bf16[128,1024]{0,1:T(8,128)(2,1)S(1)} collective-permute-done((bf16[128,1024]{0,1:T(8,128)(2,1)S(1)}, bf16[128,1024]{0,1:T(8,128)(2,1)S(1)}, u32[]{:S(2)}, u32[]{:S(2)}) %collective-permute-start) | collective-permute-done | bytes 262176 | tf_op jit(solution)/shard_map/ppermute | solution.py:19
  22.5 1.8 copy.78
  26.9 1.2 reduce.20
  29.7 5.0 %collective-permute-start.1 = (bf16[64,1024]{0,1:T(8,128)(2,1)S(1)}, bf16[64,1024]{0,1:T(8,128)(2,1)S(1)}, u32[]{:S(2)}, u32[]{:S(2)}) collective-permute-start(bf16[64,1024]{0,1:T(8,128)(2,1)S(1)} %get-tuple-element.327), channel_id=1, source_target_pairs={{0,1},{1,2},{2,3},{3,4},{4,5},{5,6},{6,7},{7,8},{8,9},{9,10},{10,1... | collective-permute-start | bytes 393224 | tf_op jit(solution)/shard_map/ppermute | solution.py:27
  34.7 1.9 collective-permute-start.2
  36.6 39.2 %all-gather.2 = bf16[1,4096]{1,0:T(2,128)(2,1)S(1)} all-gather(bf16[1,128]{1,0:T(2,128)(2,1)S(1)} %get-tuple-element.331), channel_id=4, replica_groups=mesh['pipe'=8,'ctx'=32] {'ctx'}, dimensions={1}, use_global_device_ids=true | all-gather | bytes 8448 | tf_op jit(solution)/shard_map/all_gather | solution.py:165
  75.9 30.5 %all-gather.1 = f32[1,4096]{1,0:T(1,128)S(1)} all-gather(f32[1,128]{1,0:T(1,128)S(1)} %get-tuple-element.333), channel_id=3, replica_groups=mesh['pipe'=8,'ctx'=32] {'ctx'}, dimensions={1}, use_global_device_ids=true | all-gather | bytes 16896 | tf_op jit(solution)/shard_map/all_gather | solution.py:185
  107.6 2.3 copy.76
  115.3 2.0 fusion.93
  118.2 65.1 %while.26 = (s32[]{:T(128)}, f32[128,16]{0,1:T(8,128)S(1)}, f32[128,16]{0,1:T(8,128)S(1)}, f32[128,16]{0,1:T(8,128)S(1)}, bf16[8,512]{1,0:T(8,128)(2,1)S(1)}, /*...) while((s32[]{:T(128)}, f32[128,16]{0,1:T(8,128)S(1)}, ...), condition=%wide.region_4.5_spmd.clone, body=%wide.region_0.4_spmd.clone.sunk | while | flops 284768768 | bytes 24049328 | solution.py:171
  120.4 1.3 constant_dynamic-slice_fusion.10
  123.9 1.6 fusion.131
  128.6 1.3 constant_dynamic-slice_fusion.10
  132.0 1.6 fusion.131
  136.7 1.3 constant_dynamic-slice_fusion.10
  140.1 1.6 fusion.131
  144.9 1.3 constant_dynamic-slice_fusion.10
  148.3 1.6 fusion.131
  153.0 1.3 constant_dynamic-slice_fusion.10
  156.4 1.6 fusion.131
  161.1 1.3 constant_dynamic-slice_fusion.10
  164.5 1.6 fusion.131
  169.3 1.3 constant_dynamic-slice_fusion.10
  172.7 1.6 fusion.131
  177.4 1.3 constant_dynamic-slice_fusion.10
  180.8 1.6 fusion.131
  183.4 33.4 %all_gather.27 = f32[4096,16]{0,1:T(8,128)S(1)} all-gather(f32[128,16]{0,1:T(8,128)S(1)} %get-tuple-element.329), channel_id=1, replica_groups=mesh['pipe'=8,'ctx'=32] {'ctx'}, dimensions={0}, use_global_device_ids=true | all-gather | bytes 270336 | tf_op jit(solution)/shard_map/all_gather | solution.py:184
  217.6 32.4 %all_gather.25 = f32[4096,16]{0,1:T(8,128)S(1)} all-gather(f32[128,16]{0,1:T(8,128)S(1)} %get-tuple-element.330), channel_id=1, replica_groups=mesh['pipe'=8,'ctx'=32] {'ctx'}, dimensions={0}, use_global_device_ids=true | all-gather | bytes 270336 | tf_op jit(solution)/shard_map/all_gather | solution.py:183
  250.9 12.0 %copy.80 = bf16[4096,1024]{1,0:T(8,128)(2,1)} copy(bf16[4096,1024]{0,1:T(8,128)(2,1)} %all-gather.8.cloned.1.call-done) | data formatting | bytes 16777216 | tf_op jit(solution)/shard_map/all_gather | solution.py:211
  262.9 140.5 %while.27 = (s32[]{:T(128)}, f32[128,1024]{0,1:T(8,128)}, bf16[8,512,1024]{2,1,0:T(8,128)(2,1)}, f32[128]{0:T(128)S(1)}, f32[8,512]{1,0:T(8,128)}, /*index=5*/bf...) while((s32[]{:T(128)}, f32[128,1024]{0,1:T(8,128)}, ...), condition=%wide.region_6.7_spmd.clone, body=%wide.region_5.6_spmd.clone.sunk | while | flops 548339712 | bytes 35699416 | solution.py:223
  264.9 1.7 constant_dynamic-slice_fusion.11
  267.7 2.8 fusion.141
  270.4 5.4 %fusion.142 = f32[16,64,128]{2,1,0:T(8,128)S(1)} fusion(bf16[512,16,64]{0,2,1:T(8,128)(2,1)S(1)} %bitcast.339, f32[16,512,128]{2,1,0:T(8,128)} %fusion.141, bf16[512,16,64]{0,2,1:T(8,128)(2,1)S(1)} %bitcast.340, bf16[128,16,64]{0,2,1:T(8,128)(2,1)} %get-tuple-element.576, f32[512,16]{0,1:T(8,128)S(1)} %bitcast.359, f32[512,16]{0,1:T(8,128)S(1)} %bitcast.357, ...), kind=kOutput, calls=%fused_computation.13.clone.1 | convolution fusion | flops 274857984 | bytes 7208960 | tf_op jit(solution)/shard_map/while/body/eval_jaxpr/qhk,qhe->khe/dot_general | solution.py:114
  275.8 3.2 fusion.143
  282.4 1.8 constant_dynamic-slice_fusion.11
  285.3 2.8 fusion.141
  288.0 5.4 %fusion.142 = f32[16,64,128]{2,1,0:T(8,128)S(1)} fusion(bf16[512,16,64]{0,2,1:T(8,128)(2,1)S(1)} %bitcast.339, f32[16,512,128]{2,1,0:T(8,128)} %fusion.141, bf16[512,16,64]{0,2,1:T(8,128)(2,1)S(1)} %bitcast.340, bf16[128,16,64]{0,2,1:T(8,128)(2,1)} %get-tuple-element.576, f32[512,16]{0,1:T(8,128)S(1)} %bitcast.359, f32[512,16]{0,1:T(8,128)S(1)} %bitcast.357, ...), kind=kOutput, calls=%fused_computation.13.clone.1 | convolution fusion | flops 274857984 | bytes 7208960 | tf_op jit(solution)/shard_map/while/body/eval_jaxpr/qhk,qhe->khe/dot_general | solution.py:114
  293.4 3.2 fusion.143
  300.0 1.7 constant_dynamic-slice_fusion.11
  302.8 2.8 fusion.141
  305.6 5.4 %fusion.142 = f32[16,64,128]{2,1,0:T(8,128)S(1)} fusion(bf16[512,16,64]{0,2,1:T(8,128)(2,1)S(1)} %bitcast.339, f32[16,512,128]{2,1,0:T(8,128)} %fusion.141, bf16[512,16,64]{0,2,1:T(8,128)(2,1)S(1)} %bitcast.340, bf16[128,16,64]{0,2,1:T(8,128)(2,1)} %get-tuple-element.576, f32[512,16]{0,1:T(8,128)S(1)} %bitcast.359, f32[512,16]{0,1:T(8,128)S(1)} %bitcast.357, ...), kind=kOutput, calls=%fused_computation.13.clone.1 | convolution fusion | flops 274857984 | bytes 7208960 | tf_op jit(solution)/shard_map/while/body/eval_jaxpr/qhk,qhe->khe/dot_general | solution.py:114
  310.9 3.2 fusion.143
  317.6 1.7 constant_dynamic-slice_fusion.11
  320.4 2.8 fusion.141
  323.1 5.4 %fusion.142 = f32[16,64,128]{2,1,0:T(8,128)S(1)} fusion(bf16[512,16,64]{0,2,1:T(8,128)(2,1)S(1)} %bitcast.339, f32[16,512,128]{2,1,0:T(8,128)} %fusion.141, bf16[512,16,64]{0,2,1:T(8,128)(2,1)S(1)} %bitcast.340, bf16[128,16,64]{0,2,1:T(8,128)(2,1)} %get-tuple-element.576, f32[512,16]{0,1:T(8,128)S(1)} %bitcast.359, f32[512,16]{0,1:T(8,128)S(1)} %bitcast.357, ...), kind=kOutput, calls=%fused_computation.13.clone.1 | convolution fusion | flops 274857984 | bytes 7208960 | tf_op jit(solution)/shard_map/while/body/eval_jaxpr/qhk,qhe->khe/dot_general | solution.py:114
  328.5 3.2 fusion.143
  335.1 1.7 constant_dynamic-slice_fusion.11
  337.9 2.8 fusion.141
  340.7 5.4 %fusion.142 = f32[16,64,128]{2,1,0:T(8,128)S(1)} fusion(bf16[512,16,64]{0,2,1:T(8,128)(2,1)S(1)} %bitcast.339, f32[16,512,128]{2,1,0:T(8,128)} %fusion.141, bf16[512,16,64]{0,2,1:T(8,128)(2,1)S(1)} %bitcast.340, bf16[128,16,64]{0,2,1:T(8,128)(2,1)} %get-tuple-element.576, f32[512,16]{0,1:T(8,128)S(1)} %bitcast.359, f32[512,16]{0,1:T(8,128)S(1)} %bitcast.357, ...), kind=kOutput, calls=%fused_computation.13.clone.1 | convolution fusion | flops 274857984 | bytes 7208960 | tf_op jit(solution)/shard_map/while/body/eval_jaxpr/qhk,qhe->khe/dot_general | solution.py:114
  346.1 3.2 fusion.143
  352.7 1.7 constant_dynamic-slice_fusion.11
  355.5 2.8 fusion.141
  358.3 5.4 %fusion.142 = f32[16,64,128]{2,1,0:T(8,128)S(1)} fusion(bf16[512,16,64]{0,2,1:T(8,128)(2,1)S(1)} %bitcast.339, f32[16,512,128]{2,1,0:T(8,128)} %fusion.141, bf16[512,16,64]{0,2,1:T(8,128)(2,1)S(1)} %bitcast.340, bf16[128,16,64]{0,2,1:T(8,128)(2,1)} %get-tuple-element.576, f32[512,16]{0,1:T(8,128)S(1)} %bitcast.359, f32[512,16]{0,1:T(8,128)S(1)} %bitcast.357, ...), kind=kOutput, calls=%fused_computation.13.clone.1 | convolution fusion | flops 274857984 | bytes 7208960 | tf_op jit(solution)/shard_map/while/body/eval_jaxpr/qhk,qhe->khe/dot_general | solution.py:114
  363.6 3.2 fusion.143
  370.2 1.7 constant_dynamic-slice_fusion.11
  373.1 2.8 fusion.141
  375.8 5.4 %fusion.142 = f32[16,64,128]{2,1,0:T(8,128)S(1)} fusion(bf16[512,16,64]{0,2,1:T(8,128)(2,1)S(1)} %bitcast.339, f32[16,512,128]{2,1,0:T(8,128)} %fusion.141, bf16[512,16,64]{0,2,1:T(8,128)(2,1)S(1)} %bitcast.340, bf16[128,16,64]{0,2,1:T(8,128)(2,1)} %get-tuple-element.576, f32[512,16]{0,1:T(8,128)S(1)} %bitcast.359, f32[512,16]{0,1:T(8,128)S(1)} %bitcast.357, ...), kind=kOutput, calls=%fused_computation.13.clone.1 | convolution fusion | flops 274857984 | bytes 7208960 | tf_op jit(solution)/shard_map/while/body/eval_jaxpr/qhk,qhe->khe/dot_general | solution.py:114
  381.2 3.2 fusion.143
  387.8 1.7 constant_dynamic-slice_fusion.11
  390.6 2.8 fusion.141
  393.4 5.4 %fusion.142 = f32[16,64,128]{2,1,0:T(8,128)S(1)} fusion(bf16[512,16,64]{0,2,1:T(8,128)(2,1)S(1)} %bitcast.339, f32[16,512,128]{2,1,0:T(8,128)} %fusion.141, bf16[512,16,64]{0,2,1:T(8,128)(2,1)S(1)} %bitcast.340, bf16[128,16,64]{0,2,1:T(8,128)(2,1)} %get-tuple-element.576, f32[512,16]{0,1:T(8,128)S(1)} %bitcast.359, f32[512,16]{0,1:T(8,128)S(1)} %bitcast.357, ...), kind=kOutput, calls=%fused_computation.13.clone.1 | convolution fusion | flops 274857984 | bytes 7208960 | tf_op jit(solution)/shard_map/while/body/eval_jaxpr/qhk,qhe->khe/dot_general | solution.py:114
  398.7 3.2 fusion.143
  404.6 1.8 fusion.37
  (316 shorter events, 96.5 us)
Async XLA Ops:
  6.5 111.7 %all-gather.12.cloned.1.call-start = ((), (), s32[]{:S(2)}) async-start(), calls=%async_computation.2 | async-start | bytes 8650752 | tf_op jit(solution)/shard_map/all_gather | solution.py:164
  7.3 243.6 %all-gather.8.cloned.1.call-start = ((), (), s32[]{:S(2)}) async-start(), calls=%async_computation | async-start | bytes 8650752 | tf_op jit(solution)/shard_map/all_gather | solution.py:211
  8.4 11.5 %collective-permute-start = (bf16[128,1024]{0,1:T(8,128)(2,1)S(1)}, bf16[128,1024]{0,1:T(8,128)(2,1)S(1)}, u32[]{:S(2)}, u32[]{:S(2)}) collective-permute-start(bf16[128,1024]{0,1:T(8,128)(2,1)S(1)} %bitcast.363), channel_id=1, source_target_pairs={{32,0},{64,32},{96,64},{128,96},{160,128},{192,160},{224,192},{33,... | collective-permute-start | bytes 786440 | tf_op jit(solution)/shard_map/ppermute | solution.py:19
  20.6 91.2 %copy-start.2 = (bf16[128,1024]{0,1:T(8,128)(2,1)S(1)}, bf16[128,1024]{0,1:T(8,128)(2,1)}, u32[]{:S(2)}) copy-start(bf16[128,1024]{0,1:T(8,128)(2,1)} %broadcast_select_fusion) | copy-start | bytes 786436
  20.7 242.2 %all-gather.10.cloned.1.call-start = ((), (), s32[]{:S(2)}) async-start(), calls=%async_computation.1 | async-start | bytes 8650752 | tf_op jit(solution)/shard_map/all_gather | solution.py:210
  29.7 82.0 %collective-permute-start.1 = (bf16[64,1024]{0,1:T(8,128)(2,1)S(1)}, bf16[64,1024]{0,1:T(8,128)(2,1)S(1)}, u32[]{:S(2)}, u32[]{:S(2)}) collective-permute-start(bf16[64,1024]{0,1:T(8,128)(2,1)S(1)} %get-tuple-element.327), channel_id=1, source_target_pairs={{0,1},{1,2},{2,3},{3,4},{4,5},{5,6},{6,7},{7,8},{8,9},{9,10},{10,1... | collective-permute-start | bytes 393224 | tf_op jit(solution)/shard_map/ppermute | solution.py:27
  34.7 77.1 %collective-permute-start.2 = (bf16[64,1024]{0,1:T(8,128)(2,1)S(1)}, bf16[64,1024]{0,1:T(8,128)(2,1)S(1)}, u32[]{:S(2)}, u32[]{:S(2)}) collective-permute-start(bf16[64,1024]{0,1:T(8,128)(2,1)S(1)} %get-tuple-element.328), channel_id=1, source_target_pairs={{1,0},{2,1},{3,2},{4,3},{5,4},{6,5},{7,6},{8,7},{9,8},{10,9},{11,1... | collective-permute-start | bytes 393224 | tf_op jit(solution)/shard_map/ppermute | solution.py:30
  113.8 1.5 copy-start.3
  115.0 3.3 copy-start.4
  115.0 3.3 copy-start.5
  115.0 3.3 copy-start.6
  270.4 8.7 %copy-start = (f32[128,1024]{0,1:T(8,128)S(1)}, f32[128,1024]{0,1:T(8,128)}, u32[]{:S(2)}) copy-start(f32[128,1024]{0,1:T(8,128)} %get-tuple-element.555) | copy-start | bytes 1572868 | tf_op jit(solution)/shard_map/while
  279.6 0.8 copy-start.1
  288.0 8.7 %copy-start = (f32[128,1024]{0,1:T(8,128)S(1)}, f32[128,1024]{0,1:T(8,128)}, u32[]{:S(2)}) copy-start(f32[128,1024]{0,1:T(8,128)} %get-tuple-element.555) | copy-start | bytes 1572868 | tf_op jit(solution)/shard_map/while
  297.2 0.8 copy-start.1
  305.6 8.7 %copy-start = (f32[128,1024]{0,1:T(8,128)S(1)}, f32[128,1024]{0,1:T(8,128)}, u32[]{:S(2)}) copy-start(f32[128,1024]{0,1:T(8,128)} %get-tuple-element.555) | copy-start | bytes 1572868 | tf_op jit(solution)/shard_map/while
  314.8 0.8 copy-start.1
  323.1 8.7 %copy-start = (f32[128,1024]{0,1:T(8,128)S(1)}, f32[128,1024]{0,1:T(8,128)}, u32[]{:S(2)}) copy-start(f32[128,1024]{0,1:T(8,128)} %get-tuple-element.555) | copy-start | bytes 1572868 | tf_op jit(solution)/shard_map/while
  332.3 0.8 copy-start.1
  340.7 8.7 %copy-start = (f32[128,1024]{0,1:T(8,128)S(1)}, f32[128,1024]{0,1:T(8,128)}, u32[]{:S(2)}) copy-start(f32[128,1024]{0,1:T(8,128)} %get-tuple-element.555) | copy-start | bytes 1572868 | tf_op jit(solution)/shard_map/while
  349.9 0.8 copy-start.1
  358.3 8.7 %copy-start = (f32[128,1024]{0,1:T(8,128)S(1)}, f32[128,1024]{0,1:T(8,128)}, u32[]{:S(2)}) copy-start(f32[128,1024]{0,1:T(8,128)} %get-tuple-element.555) | copy-start | bytes 1572868 | tf_op jit(solution)/shard_map/while
  367.5 0.8 copy-start.1
  375.8 8.7 %copy-start = (f32[128,1024]{0,1:T(8,128)S(1)}, f32[128,1024]{0,1:T(8,128)}, u32[]{:S(2)}) copy-start(f32[128,1024]{0,1:T(8,128)} %get-tuple-element.555) | copy-start | bytes 1572868 | tf_op jit(solution)/shard_map/while
  385.0 0.8 copy-start.1
  393.4 8.7 %copy-start = (f32[128,1024]{0,1:T(8,128)S(1)}, f32[128,1024]{0,1:T(8,128)}, u32[]{:S(2)}) copy-start(f32[128,1024]{0,1:T(8,128)} %get-tuple-element.555) | copy-start | bytes 1572868 | tf_op jit(solution)/shard_map/while
  402.6 0.8 copy-start.1
Sparse Core Ops, SparseCore 0:
  9.2 76.3 all-gather.11
  87.3 89.5 all-gather.7
  178.8 70.4 all-gather.9
where the time goes:
time: 415 us; the launch traced here: 413 us
  blocking collectives  135 us (33%)
  matrix products  114 us (27%)
  local copies, waits for them, and re-layouts  94.4 us (23%)
  other arithmetic  34.7 us (8%)
  between operations  13.6 us (3%)
  starting transfers between devices  9.84 us (2%)
  waiting for transfers between devices  8.88 us (2%)
    dot_general x8, matrix products, key_terms(): jnp.einsum('qhk,qhe->khe', score_grad, query_heads, preferred_element_typ...  42.9 us
    all_gather x1, blocking collectives, on_device(): lax.all_gather(time_wire, 'ctx', axis=0, tiled=True)  39.2 us
    dynamic_slice x40, local copies, waits for them, and re-layouts, on_device(): lax.scan(sweep_keys, running, (segment_x.reshape(length // block_size, bl...  37.2 us
    all_gather x1, blocking collectives, on_device(): lax.all_gather(delta_rows, 'ctx', axis=0, tiled=True)  33.4 us
    all_gather x1, blocking collectives, on_device(): lax.all_gather(log_total, 'ctx', axis=0, tiled=True)  32.4 us
    dot_general x16, matrix products, masked_scores(): jnp.einsum('qhe,khe->qhk', query_heads, key_heads, preferred_element_type...  31.2 us
    all_gather x1, blocking collectives, on_device(): lax.all_gather(own_times, 'ctx', axis=0, tiled=True)  30.5 us
    dot_general x8, matrix products, key_terms(): jnp.einsum('qhk,qhe->khe', probability.astype(jnp.bfloat16), grad_heads,...  25.7 us
  transfers between devices with their start and end apart: 6, of which 1 were waited for; matrix products, arithmetic and copies ran while one was open for 24% of the time, Pallas kernels for 0%

commit v1 on v0

--- a/solution.py
+++ b/solution.py
@@ -11,6 +11,13 @@
 GZ = 8
 D = 1024
 FIELDS = 8
+
+
+def all_by_exchange(value, axis, dim):
+    size = lax.axis_size(axis)
+    blocks = jnp.stack([value for _ in range(size)])
+    blocks = lax.all_to_all(blocks, axis, split_axis=0, concat_axis=0)
+    return jnp.concatenate(blocks, axis=dim)
 
 
 def shifted(value, axis, steps):
@@ -208,7 +215,7 @@
     accumulated = jnp.zeros((row_count, feature_count), jnp.float32)
     shard_part = (
         lax.all_gather(own_queries, "ctx", axis=0, tiled=True),
-        lax.all_gather(incoming, "ctx", axis=0, tiled=True),
+        all_by_exchange(incoming, "ctx", 0),
     )
     length = shard_part[0].shape[0]
     block_size = math.gcd(length, 512)

time: 415 us -> 560 us (1.35)
  blocking collectives: 135 us -> 221 us
  matrix products: 114 us -> 162 us
  other arithmetic: 34.7 us -> 57.4 us
  local copies, waits for them, and re-layouts: 94.4 us -> 82.4 us
  waiting for transfers between devices: 8.88 us -> 0.74 us
    all_gather x1, blocking collectives: 32.4 us -> 122 us  [on_device(): lax.all_gather(log_total, 'ctx', axis=0, tiled=True)]
    dot_general x16, matrix products: 31.2 us -> 55.1 us  [masked_scores(): jnp.einsum('qhe,khe->qhk', query_heads, key_heads, preferred_element_type...]
    reduce_sum x8, other arithmetic: 7.07 us -> 24.4 us  [running_stats(): jnp.sum(exponent, axis=2)]
    dot_general x8, matrix products: 12.8 us -> 29.8 us  [running_stats(): jnp.einsum('qhe,khe->qhk', grad_heads, value_heads, preferred_element_typ...]
    all_gather x1 -> x0, local copies, waits for them, and re-layouts: 12 us -> none  [on_device(): lax.all_gather(incoming, 'ctx', axis=0, tiled=True)]
    add x8, other arithmetic: 4.1 us -> 12.6 us  [sweep_queries(): accumulated + key_terms(split_heads(segment_q), split_heads(segment_g), s...]
    ppermute x1, waiting for transfers between devices: 7.46 us -> 0.01 us  [shifted(): lax.ppermute(value, axis, [(source, source + steps) for source in range(l...]
    dot_general x8, matrix products: 42.9 us -> 49.8 us  [key_terms(): jnp.einsum('qhk,qhe->khe', score_grad, query_heads, preferred_element_typ...]
  transfers between devices with their start and end apart: 6 -> 6, of which waited for: 1 -> 0; matrix products, arithmetic and copies ran while one was open for 24% -> 26% of each run, Pallas kernels for 0% -> 0%
where the time goes in v1:
time: 560 us; the launch traced here: 554 us
  blocking collectives  221 us (39%)
  matrix products  162 us (29%)
  local copies, waits for them, and re-layouts  82.4 us (15%)
  other arithmetic  57.4 us (10%)
  starting transfers between devices  15.1 us (3%)
  between operations  13.8 us (2%)
    all_gather x1, blocking collectives, on_device(): lax.all_gather(log_total, 'ctx', axis=0, tiled=True)  122 us
    dot_general x16, matrix products, masked_scores(): jnp.einsum('qhe,khe->qhk', query_heads, key_heads, preferred_element_type...  55.1 us
    dot_general x8, matrix products, key_terms(): jnp.einsum('qhk,qhe->khe', score_grad, query_heads, preferred_element_typ...  49.8 us
    dynamic_slice x40, local copies, waits for them, and re-layouts, on_device(): lax.scan(sweep_keys, running, (segment_x.reshape(length // block_size, bl...  37.1 us
    all_gather x1, blocking collectives, on_device(): lax.all_gather(time_wire, 'ctx', axis=0, tiled=True)  36.2 us
    all_gather x1, blocking collectives, on_device(): lax.all_gather(delta_rows, 'ctx', axis=0, tiled=True)  31.6 us
    all_gather x1, blocking collectives, on_device(): lax.all_gather(own_times, 'ctx', axis=0, tiled=True)  30.4 us
    dot_general x8, matrix products, running_stats(): jnp.einsum('qhe,khe->qhk', grad_heads, value_heads, preferred_element_typ...  29.8 us
  transfers between devices with their start and end apart: 6, of which 0 were waited for; matrix products, arithmetic and copies ran while one was open for 26% of the time, Pallas kernels for 0%

profile of v1, /device:TPU:29, one launch (start us, length us, event | category | flops | bytes accessed | tf_op | source)
XLA Modules:
  0.0 554.2 jit_solution(10740507614252324934)
XLA Ops:
  7.3 2.9 collective-permute-start
  15.8 1.8 copy.38
  17.6 1.9 copy.36
  19.6 4.4 collective-permute-start.1
  24.0 1.9 collective-permute-start.2
  26.0 36.2 %all-gather.2 = bf16[1,4096]{1,0:T(2,128)(2,1)S(1)} all-gather(bf16[1,128]{1,0:T(2,128)(2,1)S(1)} %get-tuple-element.308), channel_id=4, replica_groups=mesh['pipe'=8,'ctx'=32] {'ctx'}, dimensions={1}, use_global_device_ids=true | all-gather | bytes 8448 | tf_op jit(solution)/shard_map/all_gather | solution.py:172
  63.5 30.4 %all-gather.1 = f32[1,4096]{1,0:T(1,128)S(1)} all-gather(f32[1,128]{1,0:T(1,128)S(1)} %get-tuple-element.310), channel_id=3, replica_groups=mesh['pipe'=8,'ctx'=32] {'ctx'}, dimensions={1}, use_global_device_ids=true | all-gather | bytes 16896 | tf_op jit(solution)/shard_map/all_gather | solution.py:192
  96.1 4.3 stack.147
  100.4 5.8 %all-to-all-start = ((bf16[32,128,1024]{2,1,0:T(8,128)(2,1)}), bf16[32,128,1024]{2,1,0:T(8,128)(2,1)}, u32[]{:S(2)}, u32[]{:S(2)}) async-start(bf16[32,128,1024]{2,1,0:T(8,128)(2,1)} %stack.147), calls=%async_computation | async-start | bytes 16777216 | tf_op jit(solution)/shard_map/all_to_all | solution.py:19
  108.6 2.0 fusion.97
  111.5 121.4 %while.26 = (s32[]{:T(128)}, f32[128,16]{0,1:T(8,128)S(1)}, f32[128,16]{0,1:T(8,128)S(1)}, f32[128,16]{0,1:T(8,128)S(1)}, bf16[8,512]{1,0:T(8,128)(2,1)S(1)}, /*...) while((s32[]{:T(128)}, f32[128,16]{0,1:T(8,128)S(1)}, ...), condition=%wide.region_4.5_spmd.clone, body=%wide.region_0.4_spmd.clone.sunk | while | flops 284768768 | bytes 25097924 | solution.py:178
  114.6 4.2 fusion.131
  118.8 3.1 fusion.135
  122.9 3.7 fusion.134
  129.8 4.2 fusion.131
  134.0 3.0 fusion.135
  138.1 3.7 fusion.134
  145.0 4.2 fusion.131
  149.1 3.0 fusion.135
  153.2 3.7 fusion.134
  160.1 4.2 fusion.131
  164.3 3.0 fusion.135
  168.4 3.7 fusion.134
  175.3 4.2 fusion.131
  179.5 3.1 fusion.135
  183.6 3.7 fusion.134
  190.5 4.2 fusion.131
  194.7 3.0 fusion.135
  198.8 3.7 fusion.134
  205.7 4.2 fusion.131
  209.9 3.0 fusion.135
  214.0 3.7 fusion.134
  220.8 4.2 fusion.131
  225.0 3.1 fusion.135
  229.1 3.7 fusion.134
  232.9 122.4 %all_gather.22 = f32[4096,16]{0,1:T(8,128)S(1)} all-gather(f32[128,16]{0,1:T(8,128)S(1)} %get-tuple-element.307), channel_id=1, replica_groups=mesh['pipe'=8,'ctx'=32] {'ctx'}, dimensions={0}, use_global_device_ids=true | all-gather | bytes 270336 | tf_op jit(solution)/shard_map/all_gather | solution.py:190
  356.2 31.6 %all_gather.23 = f32[4096,16]{0,1:T(8,128)S(1)} all-gather(f32[128,16]{0,1:T(8,128)S(1)} %get-tuple-element.306), channel_id=1, replica_groups=mesh['pipe'=8,'ctx'=32] {'ctx'}, dimensions={0}, use_global_device_ids=true | all-gather | bytes 270336 | tf_op jit(solution)/shard_map/all_gather | solution.py:191
  388.7 155.6 %while.27 = (s32[]{:T(128)}, f32[128,1024]{0,1:T(8,128)}, bf16[8,512,1024]{2,1,0:T(8,128)(2,1)}, f32[128]{0:T(128)S(1)}, f32[8,512]{1,0:T(8,128)}, /*index=5*/bf...) while((s32[]{:T(128)}, f32[128,1024]{0,1:T(8,128)}, ...), condition=%wide.region_6.7_spmd.clone, body=%wide.region_5.6_spmd.clone.sunk | while | flops 548339712 | bytes 35699408 | solution.py:230
  388.7 1.7 constant_dynamic-slice_fusion.11
  390.9 2.7 fusion.144
  396.2 3.2 fusion.146
  399.5 6.2 %fusion.145 = f32[16,64,128]{2,1,0:T(8,128)} fusion(bf16[512,16,64]{0,2,1:T(8,128)(2,1)S(1)} %bitcast.339, f32[16,512,128]{2,1,0:T(8,128)} %fusion.144, bf16[512,16,64]{0,2,1:T(8,128)(2,1)S(1)} %bitcast.341, f32[512,16]{0,1:T(8,128)S(1)} %bitcast.354, f32[512,16]{0,1:T(8,128)S(1)} %bitcast.353, pred[512,128]{1,0:T(8,128)(4,1)S(1)} %broadcast_compare_fusion.5, ...), kind=kOutput, calls=%fused_computation.13.clone.1 | convolution fusion | flops 274857984 | bytes 7208960 | tf_op jit(solution)/shard_map/while/body/eval_jaxpr/qhk,qhe->khe/dot_general | solution.py:121
  410.4 2.7 fusion.144
  415.6 3.2 fusion.146
  419.0 6.2 %fusion.145 = f32[16,64,128]{2,1,0:T(8,128)} fusion(bf16[512,16,64]{0,2,1:T(8,128)(2,1)S(1)} %bitcast.339, f32[16,512,128]{2,1,0:T(8,128)} %fusion.144, bf16[512,16,64]{0,2,1:T(8,128)(2,1)S(1)} %bitcast.341, f32[512,16]{0,1:T(8,128)S(1)} %bitcast.354, f32[512,16]{0,1:T(8,128)S(1)} %bitcast.353, pred[512,128]{1,0:T(8,128)(4,1)S(1)} %broadcast_compare_fusion.5, ...), kind=kOutput, calls=%fused_computation.13.clone.1 | convolution fusion | flops 274857984 | bytes 7208960 | tf_op jit(solution)/shard_map/while/body/eval_jaxpr/qhk,qhe->khe/dot_general | solution.py:121
  429.8 2.7 fusion.144
  435.1 3.2 fusion.146
  438.4 6.2 %fusion.145 = f32[16,64,128]{2,1,0:T(8,128)} fusion(bf16[512,16,64]{0,2,1:T(8,128)(2,1)S(1)} %bitcast.339, f32[16,512,128]{2,1,0:T(8,128)} %fusion.144, bf16[512,16,64]{0,2,1:T(8,128)(2,1)S(1)} %bitcast.341, f32[512,16]{0,1:T(8,128)S(1)} %bitcast.354, f32[512,16]{0,1:T(8,128)S(1)} %bitcast.353, pred[512,128]{1,0:T(8,128)(4,1)S(1)} %broadcast_compare_fusion.5, ...), kind=kOutput, calls=%fused_computation.13.clone.1 | convolution fusion | flops 274857984 | bytes 7208960 | tf_op jit(solution)/shard_map/while/body/eval_jaxpr/qhk,qhe->khe/dot_general | solution.py:121
  449.3 2.7 fusion.144
  454.5 3.2 fusion.146
  457.9 6.2 %fusion.145 = f32[16,64,128]{2,1,0:T(8,128)} fusion(bf16[512,16,64]{0,2,1:T(8,128)(2,1)S(1)} %bitcast.339, f32[16,512,128]{2,1,0:T(8,128)} %fusion.144, bf16[512,16,64]{0,2,1:T(8,128)(2,1)S(1)} %bitcast.341, f32[512,16]{0,1:T(8,128)S(1)} %bitcast.354, f32[512,16]{0,1:T(8,128)S(1)} %bitcast.353, pred[512,128]{1,0:T(8,128)(4,1)S(1)} %broadcast_compare_fusion.5, ...), kind=kOutput, calls=%fused_computation.13.clone.1 | convolution fusion | flops 274857984 | bytes 7208960 | tf_op jit(solution)/shard_map/while/body/eval_jaxpr/qhk,qhe->khe/dot_general | solution.py:121
  468.7 2.7 fusion.144
  474.0 3.2 fusion.146
  477.3 6.2 %fusion.145 = f32[16,64,128]{2,1,0:T(8,128)} fusion(bf16[512,16,64]{0,2,1:T(8,128)(2,1)S(1)} %bitcast.339, f32[16,512,128]{2,1,0:T(8,128)} %fusion.144, bf16[512,16,64]{0,2,1:T(8,128)(2,1)S(1)} %bitcast.341, f32[512,16]{0,1:T(8,128)S(1)} %bitcast.354, f32[512,16]{0,1:T(8,128)S(1)} %bitcast.353, pred[512,128]{1,0:T(8,128)(4,1)S(1)} %broadcast_compare_fusion.5, ...), kind=kOutput, calls=%fused_computation.13.clone.1 | convolution fusion | flops 274857984 | bytes 7208960 | tf_op jit(solution)/shard_map/while/body/eval_jaxpr/qhk,qhe->khe/dot_general | solution.py:121
  488.2 2.7 fusion.144
  493.4 3.2 fusion.146
  496.8 6.2 %fusion.145 = f32[16,64,128]{2,1,0:T(8,128)} fusion(bf16[512,16,64]{0,2,1:T(8,128)(2,1)S(1)} %bitcast.339, f32[16,512,128]{2,1,0:T(8,128)} %fusion.144, bf16[512,16,64]{0,2,1:T(8,128)(2,1)S(1)} %bitcast.341, f32[512,16]{0,1:T(8,128)S(1)} %bitcast.354, f32[512,16]{0,1:T(8,128)S(1)} %bitcast.353, pred[512,128]{1,0:T(8,128)(4,1)S(1)} %broadcast_compare_fusion.5, ...), kind=kOutput, calls=%fused_computation.13.clone.1 | convolution fusion | flops 274857984 | bytes 7208960 | tf_op jit(solution)/shard_map/while/body/eval_jaxpr/qhk,qhe->khe/dot_general | solution.py:121
  507.6 2.7 fusion.144
  512.9 3.2 fusion.146
  516.2 6.2 %fusion.145 = f32[16,64,128]{2,1,0:T(8,128)} fusion(bf16[512,16,64]{0,2,1:T(8,128)(2,1)S(1)} %bitcast.339, f32[16,512,128]{2,1,0:T(8,128)} %fusion.144, bf16[512,16,64]{0,2,1:T(8,128)(2,1)S(1)} %bitcast.341, f32[512,16]{0,1:T(8,128)S(1)} %bitcast.354, f32[512,16]{0,1:T(8,128)S(1)} %bitcast.353, pred[512,128]{1,0:T(8,128)(4,1)S(1)} %broadcast_compare_fusion.5, ...), kind=kOutput, calls=%fused_computation.13.clone.1 | convolution fusion | flops 274857984 | bytes 7208960 | tf_op jit(solution)/shard_map/while/body/eval_jaxpr/qhk,qhe->khe/dot_general | solution.py:121
  527.1 2.7 fusion.144
  532.3 3.2 fusion.146
  535.7 6.2 %fusion.145 = f32[16,64,128]{2,1,0:T(8,128)} fusion(bf16[512,16,64]{0,2,1:T(8,128)(2,1)S(1)} %bitcast.339, f32[16,512,128]{2,1,0:T(8,128)} %fusion.144, bf16[512,16,64]{0,2,1:T(8,128)(2,1)S(1)} %bitcast.341, f32[512,16]{0,1:T(8,128)S(1)} %bitcast.354, f32[512,16]{0,1:T(8,128)S(1)} %bitcast.353, pred[512,128]{1,0:T(8,128)(4,1)S(1)} %broadcast_compare_fusion.5, ...), kind=kOutput, calls=%fused_computation.13.clone.1 | convolution fusion | flops 274857984 | bytes 7208960 | tf_op jit(solution)/shard_map/while/body/eval_jaxpr/qhk,qhe->khe/dot_general | solution.py:121
  545.5 1.8 fusion.39
  (321 shorter events, 104.8 us)
Async XLA Ops:
  6.5 105.0 %all-gather.9.cloned.1.call-start = ((), (), s32[]{:S(2)}) async-start(), calls=%async_computation.2 | async-start | bytes 8650752 | tf_op jit(solution)/shard_map/all_gather | solution.py:171
  7.3 381.4 %all-gather.7.cloned.1.call-start = ((), (), s32[]{:S(2)}) async-start(), calls=%async_computation.1 | async-start | bytes 8650752 | tf_op jit(solution)/shard_map/all_gather | solution.py:217
  7.3 12.2 %collective-permute-start = (bf16[128,1024]{1,0:T(8,128)(2,1)}, bf16[128,1024]{1,0:T(8,128)(2,1)S(1)}, u32[]{:S(2)}, u32[]{:S(2)}) collective-permute-start(bf16[128,1024]{1,0:T(8,128)(2,1)} %bitcast.364), channel_id=1, source_target_pairs={{32,0},{64,32},{96,64},{128,96},{160,128},{192,160},{224,192},{33,... | collective-permute-start | bytes 786440 | tf_op jit(solution)/shard_map/ppermute | solution.py:26
  19.6 86.6 %collective-permute-start.1 = (bf16[64,1024]{1,0:T(8,128)(2,1)S(1)}, bf16[64,1024]{1,0:T(8,128)(2,1)S(1)}, u32[]{:S(2)}, u32[]{:S(2)}) collective-permute-start(bf16[64,1024]{1,0:T(8,128)(2,1)S(1)} %get-tuple-element.304), channel_id=1, source_target_pairs={{0,1},{1,2},{2,3},{3,4},{4,5},{5,6},{6,7},{7,8},{8,9},{9,10},{10,1... | collective-permute-start | bytes 393224 | tf_op jit(solution)/shard_map/ppermute | solution.py:34
  24.0 82.2 %collective-permute-start.2 = (bf16[64,1024]{1,0:T(8,128)(2,1)S(1)}, bf16[64,1024]{1,0:T(8,128)(2,1)S(1)}, u32[]{:S(2)}, u32[]{:S(2)}) collective-permute-start(bf16[64,1024]{1,0:T(8,128)(2,1)S(1)} %get-tuple-element.305), channel_id=1, source_target_pairs={{1,0},{2,1},{3,2},{4,3},{5,4},{6,5},{7,6},{8,7},{9,8},{10,9},{11,1... | collective-permute-start | bytes 393224 | tf_op jit(solution)/shard_map/ppermute | solution.py:37
  100.4 288.3 %all-to-all-start = ((bf16[32,128,1024]{2,1,0:T(8,128)(2,1)}), bf16[32,128,1024]{2,1,0:T(8,128)(2,1)}, u32[]{:S(2)}, u32[]{:S(2)}) async-start(bf16[32,128,1024]{2,1,0:T(8,128)(2,1)} %stack.147), calls=%async_computation | async-start | bytes 16777216 | tf_op jit(solution)/shard_map/all_to_all | solution.py:19
  108.3 3.2 copy-start.2
  108.3 3.2 copy-start.3
  114.6 8.3 %copy-start.4 = (bf16[128,16,64]{0,2,1:T(8,128)(2,1)S(1)}, bf16[128,16,64]{0,2,1:T(8,128)(2,1)}, u32[]{:S(2)}) copy-start(bf16[128,16,64]{0,2,1:T(8,128)(2,1)} %get-tuple-element.513) | copy-start | bytes 786436 | tf_op jit(solution)/shard_map/while
  129.8 8.3 %copy-start.4 = (bf16[128,16,64]{0,2,1:T(8,128)(2,1)S(1)}, bf16[128,16,64]{0,2,1:T(8,128)(2,1)}, u32[]{:S(2)}) copy-start(bf16[128,16,64]{0,2,1:T(8,128)(2,1)} %get-tuple-element.513) | copy-start | bytes 786436 | tf_op jit(solution)/shard_map/while
  145.0 8.3 %copy-start.4 = (bf16[128,16,64]{0,2,1:T(8,128)(2,1)S(1)}, bf16[128,16,64]{0,2,1:T(8,128)(2,1)}, u32[]{:S(2)}) copy-start(bf16[128,16,64]{0,2,1:T(8,128)(2,1)} %get-tuple-element.513) | copy-start | bytes 786436 | tf_op jit(solution)/shard_map/while
  160.1 8.3 %copy-start.4 = (bf16[128,16,64]{0,2,1:T(8,128)(2,1)S(1)}, bf16[128,16,64]{0,2,1:T(8,128)(2,1)}, u32[]{:S(2)}) copy-start(bf16[128,16,64]{0,2,1:T(8,128)(2,1)} %get-tuple-element.513) | copy-start | bytes 786436 | tf_op jit(solution)/shard_map/while
  175.3 8.3 %copy-start.4 = (bf16[128,16,64]{0,2,1:T(8,128)(2,1)S(1)}, bf16[128,16,64]{0,2,1:T(8,128)(2,1)}, u32[]{:S(2)}) copy-start(bf16[128,16,64]{0,2,1:T(8,128)(2,1)} %get-tuple-element.513) | copy-start | bytes 786436 | tf_op jit(solution)/shard_map/while
  190.5 8.3 %copy-start.4 = (bf16[128,16,64]{0,2,1:T(8,128)(2,1)S(1)}, bf16[128,16,64]{0,2,1:T(8,128)(2,1)}, u32[]{:S(2)}) copy-start(bf16[128,16,64]{0,2,1:T(8,128)(2,1)} %get-tuple-element.513) | copy-start | bytes 786436 | tf_op jit(solution)/shard_map/while
  205.7 8.3 %copy-start.4 = (bf16[128,16,64]{0,2,1:T(8,128)(2,1)S(1)}, bf16[128,16,64]{0,2,1:T(8,128)(2,1)}, u32[]{:S(2)}) copy-start(bf16[128,16,64]{0,2,1:T(8,128)(2,1)} %get-tuple-element.513) | copy-start | bytes 786436 | tf_op jit(solution)/shard_map/while
  220.8 8.3 %copy-start.4 = (bf16[128,16,64]{0,2,1:T(8,128)(2,1)S(1)}, bf16[128,16,64]{0,2,1:T(8,128)(2,1)}, u32[]{:S(2)}) copy-start(bf16[128,16,64]{0,2,1:T(8,128)(2,1)} %get-tuple-element.513) | copy-start | bytes 786436 | tf_op jit(solution)/shard_map/while
  399.4 6.4 %copy-start = (f32[128,1024]{0,1:T(8,128)S(1)}, f32[128,1024]{0,1:T(8,128)}, u32[]{:S(2)}) copy-start(f32[128,1024]{0,1:T(8,128)} %get-tuple-element.532) | copy-start | bytes 1572868 | tf_op jit(solution)/shard_map/while
  407.3 0.8 copy-start.1
  418.8 6.4 %copy-start = (f32[128,1024]{0,1:T(8,128)S(1)}, f32[128,1024]{0,1:T(8,128)}, u32[]{:S(2)}) copy-start(f32[128,1024]{0,1:T(8,128)} %get-tuple-element.532) | copy-start | bytes 1572868 | tf_op jit(solution)/shard_map/while
  426.8 0.8 copy-start.1
  438.3 6.4 %copy-start = (f32[128,1024]{0,1:T(8,128)S(1)}, f32[128,1024]{0,1:T(8,128)}, u32[]{:S(2)}) copy-start(f32[128,1024]{0,1:T(8,128)} %get-tuple-element.532) | copy-start | bytes 1572868 | tf_op jit(solution)/shard_map/while
  446.2 0.8 copy-start.1
  457.7 6.4 %copy-start = (f32[128,1024]{0,1:T(8,128)S(1)}, f32[128,1024]{0,1:T(8,128)}, u32[]{:S(2)}) copy-start(f32[128,1024]{0,1:T(8,128)} %get-tuple-element.532) | copy-start | bytes 1572868 | tf_op jit(solution)/shard_map/while
  465.7 0.8 copy-start.1
  477.2 6.4 %copy-start = (f32[128,1024]{0,1:T(8,128)S(1)}, f32[128,1024]{0,1:T(8,128)}, u32[]{:S(2)}) copy-start(f32[128,1024]{0,1:T(8,128)} %get-tuple-element.532) | copy-start | bytes 1572868 | tf_op jit(solution)/shard_map/while
  485.1 0.8 copy-start.1
  496.6 6.4 %copy-start = (f32[128,1024]{0,1:T(8,128)S(1)}, f32[128,1024]{0,1:T(8,128)}, u32[]{:S(2)}) copy-start(f32[128,1024]{0,1:T(8,128)} %get-tuple-element.532) | copy-start | bytes 1572868 | tf_op jit(solution)/shard_map/while
  504.6 0.8 copy-start.1
  516.1 6.4 %copy-start = (f32[128,1024]{0,1:T(8,128)S(1)}, f32[128,1024]{0,1:T(8,128)}, u32[]{:S(2)}) copy-start(f32[128,1024]{0,1:T(8,128)} %get-tuple-element.532) | copy-start | bytes 1572868 | tf_op jit(solution)/shard_map/while
  524.0 0.8 copy-start.1
  535.6 6.4 %copy-start = (f32[128,1024]{0,1:T(8,128)S(1)}, f32[128,1024]{0,1:T(8,128)}, u32[]{:S(2)}) copy-start(f32[128,1024]{0,1:T(8,128)} %get-tuple-element.532) | copy-start | bytes 1572868 | tf_op jit(solution)/shard_map/while
  543.5 0.8 copy-start.1
Sparse Core Ops, SparseCore 0:
  9.2 75.7 all-gather.8
  86.8 178.4 all-gather.6
